TPU v7x, 32 devices: a whole 2x2x4 slice. The times are simulated.
32 devices in a mesh: expert: 8 (over z, y), replica: 4 (over x, core).
Axes of the slice: x: 2, y: 2, z: 4, core: 2. Of those that a mesh axis runs over, the one named last changes fastest.
Arguments:
- tokens: bfloat16 [8192, 7168], P(('expert', 'replica')), may hold values from -6 to 6
- routes: int32 [8192, 8], P(('expert', 'replica')), may hold values from 0 to 255, all different within a row
- counts: int32 [32], P(('expert', 'replica')), may hold values from 128 to 256, as said below
- w_gate: bfloat16 [8, 7168, 2048], P('expert', None, 'replica'), may hold values from -0.0625 to 0.0625
- w_up: bfloat16 [8, 7168, 2048], P('expert', None, 'replica'), may hold values from -0.0625 to 0.0625
Outputs:
- key_cov: float32 [8, 2048, 2048], P('expert', 'replica')
Inputs may be any that keep to these rules, and one draw needn't show every extreme that they name: `counts`: every count is a multiple of 128; some device has 256 and some 128.
All inputs are finite; a program needn't handle non-finite values.
Results may differ from a plain program's by a relative error of at most 0.0039.
Values may be sent and summed in bfloat16 or wider, within the bound.
A program may use at most 128 MiB of HBM per device.

v0:
```python
import jax
import jax.numpy as jnp
from jax import lax
from jax.sharding import PartitionSpec as P

N_ROUTED = 256
TOP = 8


def slot_tokens(route_block, real_count, expert_total, capacity):
    flat_route = route_block.reshape(-1)
    position = jnp.arange(flat_route.shape[0], dtype=jnp.int32)
    owner_token = position // TOP
    usable = (owner_token < real_count) & (flat_route < expert_total)
    hit_table = (
        (flat_route[:, None] == jnp.arange(expert_total, dtype=jnp.int32)[None, :])
        & usable[:, None]
    ).astype(jnp.int32)
    slot_rank = jnp.sum((jnp.cumsum(hit_table, axis=0) - hit_table) * hit_table, axis=1)
    kept_slot = usable & (slot_rank < capacity)
    slot_index = flat_route * capacity + slot_rank
    slot_match = kept_slot[:, None] & (
        slot_index[:, None] == jnp.arange(expert_total * capacity, dtype=jnp.int32)[None, :]
    )
    filled = jnp.any(slot_match, axis=0)
    source = jnp.sum(jnp.where(slot_match, owner_token[:, None], 0), axis=0)
    return (source, filled)


def body(tokens, routes, counts, w_gate, w_up):
    expert_count = lax.axis_size("expert")
    replica_count = lax.axis_size("replica")
    slot_total, width_model = tokens.shape
    capacity = slot_total * TOP // N_ROUTED
    source, filled = slot_tokens(routes, counts[0], expert_count, capacity)
    slot_rows = jnp.where(filled[:, None], tokens[source], jnp.zeros((), tokens.dtype))
    slot_rows = slot_rows.reshape(expert_count, capacity, width_model)
    gate_matrix = w_gate[0]
    up_matrix = w_up[0]
    replicas = jnp.broadcast_to(
        slot_rows[:, None], (expert_count, replica_count, capacity, width_model)
    )
    replicas = replicas.reshape(expert_count * replica_count, capacity, width_model)
    slot_block = lax.all_to_all(
        replicas, ("expert", "replica"), split_axis=0, concat_axis=0, tiled=True
    )
    gate_pre = jnp.einsum(
        "sce,ef->scf", slot_block, gate_matrix, preferred_element_type=jnp.float32
    )
    up_pre = jnp.einsum("sce,ef->scf", slot_block, up_matrix, preferred_element_type=jnp.float32)
    exchanged = (jax.nn.silu(gate_pre) * up_pre).astype(jnp.bfloat16)
    own_keys = exchanged.reshape(expert_count * replica_count * capacity, exchanged.shape[2])
    factor = 1.0 / (expert_count * capacity)
    key_gram = (
        jnp.einsum(
            "rf,rg->fg",
            own_keys,
            lax.all_gather(own_keys, "replica", axis=1, tiled=True),
            preferred_element_type=jnp.float32,
        )
        * factor
    )
    return key_gram[None]


def solution(mesh):
    return jax.shard_map(
        body,
        mesh=mesh,
        in_specs=(
            P(("expert", "replica"), None),
            P(("expert", "replica"), None),
            P(("expert", "replica")),
            P("expert", None, "replica"),
            P("expert", None, "replica"),
        ),
        out_specs=P("expert", "replica", None),
        check_vma=False,
    )
```

profile of v0, /device:TPU:0, one launch (start us, length us, event | category | flops | bytes accessed | tf_op | source)
XLA Modules:
  0.0 141.3 jit_solution(12893401506490114549)
XLA Ops:
  6.5 0.0 all-gather.2.cloned.1.call-start
  6.5 0.8 copy.8
  7.4 0.1 reshape.100
  7.5 0.1 eq.39
  8.3 2.3 %reduce-window.6 = s32[8,16,128]{2,1,0:T(8,128)S(1)} reduce-window(s32[8,16,128]{2,1,0:T(8,128)S(1)} %fusion.20, s32[]{:T(128)} %constant.35.clone.1), window={size=1x1x128 pad=0_0x0_0x127_0}, to_apply=%region_0.1 | reduce-window | flops 2080768 | bytes 131076 | tf_op jit(solution)/shard_map/reduce-window
  10.6 0.3 slice_reduce_fusion
  10.9 0.2 reduce-window.9
  11.0 0.1 add_bitcast_fusion
  11.2 0.2 fusion.14
  11.4 0.2 select_reduce_fusion
  11.6 0.1 broadcast_in_dim.42
  11.7 4.5 %gather_fusion = bf16[64,7168]{1,0:T(8,128)(2,1)S(1)} fusion(bf16[256,7168]{1,0:T(8,128)(2,1)} %param.5, s32[1024]{0:T(1024)S(1)} %pad_clamp_fusion), kind=kCustom, calls=%fused_computation | custom fusion | bytes 1835264 | tf_op jit(solution)/shard_map/gather | solution.py:36
  16.2 0.1 bitcast_select_fusion
  16.3 0.4 broadcast_in_dim.47
  16.8 0.0 slice-start
  16.8 90.1 %all_to_all.5 = bf16[32,8,7168]{2,1,0:T(8,128)(2,1)S(1)} all-to-all(bf16[32,8,7168]{2,1,0:T(8,128)(2,1)S(1)} %bitcast.52), channel_id=1, replica_groups=mesh['expert'=8,'replica'=4] {'expert','replica'}, dimensions={0} | all-to-all | bytes 7340032 | tf_op jit(solution)/shard_map/all_to_all | solution.py:44
  106.8 0.0 slice-start.1
  106.8 5.3 %fusion.2 = f32[32,8,512]{2,1,0:T(8,128)S(1)} fusion(bf16[32,8,7168]{2,1,0:T(8,128)(2,1)S(1)} %all_to_all.5, bf16[1,7168,512]{2,1,0:T(8,128)(2,1)} %param.8), kind=kOutput, calls=%fused_computation.3 | convolution fusion | flops 1879048192 | bytes 11534336 | tf_op jit(solution)/shard_map/sce,ef->scf/dot_general | solution.py:47
  112.1 0.0 slice-done
  112.1 0.0 slice-done.1
  112.1 2.8 %fusion.10 = bf16[256,512]{1,0:T(8,128)(2,1)} fusion(bf16[32,8,7168]{2,1,0:T(8,128)(2,1)S(1)} %all_to_all.5, bf16[1,7168,512]{2,1,0:T(8,128)(2,1)S(1)} %bitcast.55, f32[32,8,512]{2,1,0:T(8,128)S(1)} %fusion.2), kind=kOutput, calls=%fused_computation.8 | convolution fusion | flops 1879834624 | bytes 11796480 | tf_op jit(solution)/shard_map/sce,ef->scf/dot_general | solution.py:50
  114.9 0.0 all-gather.2.cloned.1.call-update
  115.0 15.4 %all-gather.2.cloned.1.call-done = bf16[256,2048]{1,0:T(8,128)(2,1)} async-done(((bf16[256,512]{1,0:T(8,128)(2,1)}), bf16[256,2048]{1,0:T(8,128)(2,1)}) %all-gather.2.cloned.1.call-update) | async-done | bytes 1048592 | tf_op jit(solution)/shard_map/all_gather | solution.py:58
  130.4 4.1 %multiply_bitcast_fusion = f32[1,512,2048]{2,1,0:T(8,128)} fusion(bf16[256,512]{1,0:T(8,128)(2,1)} %fusion.10, bf16[256,2048]{1,0:T(8,128)(2,1)} %all-gather.2.cloned.1.call-done), kind=kOutput, calls=%fused_computation.5 | convolution fusion | flops 537919488 | bytes 5505024 | tf_op jit(solution)/shard_map/rf,rg->fg/dot_general | solution.py:55
  (9 shorter events, 0.1 us)
Async XLA Ops:
  6.5 123.9 %all-gather.2.cloned.1.call-start = ((), (), s32[]{:S(2)}) async-start(), calls=%async_computation.1 | async-start | bytes 1310720 | tf_op jit(solution)/shard_map/all_gather | solution.py:58
  16.8 95.4 %slice-start = ((s8[7340032]{0:T(1024)(128)(4,1)}), s8[4194304]{0:T(1024)(128)(4,1)S(1)}, s32[]{:S(2)}) async-start(s8[7340032]{0:T(1024)(128)(4,1)} %bitcast.54), calls=%async_computation.2 | async-start | bytes 8388608
  106.8 5.3 %slice-start.1 = ((s8[7340032]{0:T(1024)(128)(4,1)}), s8[3145728]{0:T(1024)(128)(4,1)S(1)}, s32[]{:S(2)}) async-start(s8[7340032]{0:T(1024)(128)(4,1)} %bitcast.54), calls=%async_computation.3 | async-start | bytes 6291456
Sparse Core Ops, SparseCore 0:
  115.1 15.2 all-gather.1
where the time goes:
time: 142 us; the launch traced here: 141 us
  blocking collectives  90.1 us (63%)
  waiting for transfers between devices  15.5 us (11%)
  between operations  14.2 us (10%)
  matrix products  12.1 us (9%)
  local copies, waits for them, and re-layouts  6.31 us (4%)
  other arithmetic  3.17 us (2%)
    all_to_all x1, blocking collectives, body(): lax.all_to_all(replicas, ('expert', 'replica'), split_axis=0, concat_axis...  90.1 us
    all_gather x1, waiting for transfers between devices, body(): lax.all_gather(own_keys, 'replica', axis=1, tiled=True)  15.4 us
    dot_general x1, matrix products, body(): jnp.einsum('sce,ef->scf', slot_block, gate_matrix, preferred_element_type...  5.28 us
    gather x1, local copies, waits for them, and re-layouts, body(): tokens[source]  4.47 us
    dot_general x1, matrix products, body(): jnp.einsum('rf,rg->fg', own_keys, lax.all_gather(own_keys, 'replica', axi...  4.06 us
  transfers between devices with their start and end apart: 1, of which 1 were waited for; matrix products, arithmetic and copies ran while one was open for 0% of the time, Pallas kernels for 0%

commit v1 on v0

v1 whole, which is shorter than its diff:
```python
import functools

import jax
import jax.numpy as jnp
from jax import lax
from jax.experimental import pallas as pl
from jax.experimental.pallas import tpu as pltpu
from jax.sharding import PartitionSpec as P

N_ROUTED = 256
TOP = 8
MESH = pl.DeviceIdType.MESH


def exchange_kernel(
    sizes, counts_ref, routes_ref, tokens_hbm, gate_hbm, up_hbm, keys_ref, own_ref,
    tok, wg, wu, slots, rows, acc_g, acc_u, kbuf,
    tok_sem, wg_sem, wu_sem, a_send, a_recv, x_send, x_recv, s_send, s_recv,
    f_send, f_recv, k_send, k_recv,
):
    n_e, n_r, cap, n_tok, n_k, kc, pieces = sizes
    total_rows = n_e * n_r * cap
    piece = total_rows // pieces
    hidden = acc_g.shape[1]
    e = lax.axis_index("expert")
    r = lax.axis_index("replica")
    sib = r + 1 - 2 * (r % 2)
    across = (r + 2) % n_r

    def tok_copy(k):
        return pltpu.make_async_copy(
            tokens_hbm.at[:, pl.ds(k * kc, kc)], tok.at[k], tok_sem.at[k])

    def w_copy(hbm, buf, sem, k):
        return pltpu.make_async_copy(hbm.at[0, pl.ds(k * kc, kc), :], buf.at[k], sem.at[k])

    barrier = pltpu.get_barrier_semaphore()
    for s in range(1, n_e):
        pl.semaphore_signal(barrier, inc=1, device_id=((e + s) % n_e, r), device_id_type=MESH)
    pl.semaphore_signal(barrier, inc=1, device_id=(e, sib), device_id_type=MESH)
    pl.semaphore_signal(barrier, inc=1, device_id=(e, across), device_id_type=MESH)

    for k in range(n_k):
        tok_copy(k).start()
    for k in range(n_k):
        w_copy(gate_hbm, wg, wg_sem, k).start()
        w_copy(up_hbm, wu, wu_sem, k).start()

    n_s = n_e * cap
    count = counts_ref[0]
    slot = lax.broadcasted_iota(jnp.int32, (n_s, n_tok), 0)
    token = lax.broadcasted_iota(jnp.int32, (n_s, n_tok), 1)
    slot_expert = slot // cap
    hit = routes_ref[0:1, :] == slot_expert
    for c in range(1, TOP):
        hit = hit | (routes_ref[c:c + 1, :] == slot_expert)
    hit = hit & (token < count)
    before = lax.broadcasted_iota(jnp.int32, (n_tok, n_tok), 0) < lax.broadcasted_iota(
        jnp.int32, (n_tok, n_tok), 1)
    hit_f = jnp.where(hit, 1.0, 0.0)
    rank = jnp.dot(
        hit_f.astype(jnp.bfloat16), jnp.where(before, 1.0, 0.0).astype(jnp.bfloat16),
        preferred_element_type=jnp.float32)
    place = (slot % cap).astype(jnp.float32)
    choice = jnp.where(rank == place, hit_f, 0.0).astype(jnp.bfloat16)

    acc_g[...] = jnp.zeros_like(acc_g)
    acc_u[...] = jnp.zeros_like(acc_u)

    pl.semaphore_wait(barrier, n_e + 1)

    def a_copy(k, s):
        return pltpu.make_async_remote_copy(
            src_ref=slots.at[k, (e + s) % n_e], dst_ref=rows.at[k, r, e],
            send_sem=a_send.at[k, s], recv_sem=a_recv.at[k, s],
            device_id=((e + s) % n_e, r), device_id_type=MESH)

    def row_copy(k, who, to, send, recv):
        return pltpu.make_async_remote_copy(
            src_ref=rows.at[k, who], dst_ref=rows.at[k, who],
            send_sem=send.at[k], recv_sem=recv.at[k],
            device_id=(e, to), device_id_type=MESH)

    def x_copy(k):
        return row_copy(k, r, across, x_send, x_recv)

    def s_copy(k):
        return row_copy(k, r, sib, s_send, s_recv)

    def f_copy(k):
        return row_copy(k, across, sib, f_send, f_recv)

    half = n_e // 2
    order = sorted(range(1, n_e), key=lambda s: abs(s - half))

    @pl.loop(0, n_k)
    def _(k):
        tok_copy(k).wait()
        picked = jnp.dot(choice, tok[k], preferred_element_type=jnp.float32)
        slots[k] = picked.reshape(n_e, cap, kc).astype(jnp.bfloat16)
        for s in order:
            a_copy(k, s).start()
        rows[k, r, e] = slots[k, e]

    groups = max(1, total_rows // 256)
    per = n_r // groups
    step_rows = total_rows // groups

    @pl.loop(0, n_k + 2)
    def _(i):
        @pl.when(i < n_k)
        def _():
            for s in order:
                a_copy(i, s).wait_recv()
            x_copy(i).start()
            s_copy(i).start()

        @pl.when((i >= 1) & (i <= n_k))
        def _():
            x_copy(i - 1).wait_recv()
            f_copy(i - 1).start()

        @pl.when(i >= 2)
        def _():
            k = i - 2
            w_copy(gate_hbm, wg, wg_sem, k).wait()
            w_copy(up_hbm, wu, wu_sem, k).wait()
            s_copy(k).wait_recv()
            f_copy(k).wait_recv()
            for g in range(groups):
                block = rows[k, g * per:(g + 1) * per].reshape(step_rows, kc)
                at = slice(g * step_rows, (g + 1) * step_rows)
                acc_g[at, :] += jnp.dot(block, wg[k], preferred_element_type=jnp.float32)
                acc_u[at, :] += jnp.dot(block, wu[k], preferred_element_type=jnp.float32)

    def key_copy(p, who, to, n):
        return pltpu.make_async_remote_copy(
            src_ref=kbuf.at[p, who], dst_ref=kbuf.at[p, who],
            send_sem=k_send.at[n, p], recv_sem=k_recv.at[n, p],
            device_id=(e, to), device_id_type=MESH)

    for p in range(pieces):
        g = acc_g[p * piece:(p + 1) * piece, :]
        u = acc_u[p * piece:(p + 1) * piece, :]
        key = ((g / (1.0 + jnp.exp(-g))) * u).astype(jnp.bfloat16)
        kbuf[p, r] = key
        own_ref[p * piece:(p + 1) * piece, :] = key
        key_copy(p, r, across, 0).start()
        key_copy(p, r, sib, 1).start()
    for p in range(pieces):
        key_copy(p, r, across, 0).wait_recv()
        key_copy(p, across, sib, 2).start()
    for p in range(pieces):
        key_copy(p, r, sib, 1).wait_recv()
        key_copy(p, across, sib, 2).wait_recv()
        for q in range(n_r):
            keys_ref[p * piece:(p + 1) * piece, q * hidden:(q + 1) * hidden] = kbuf[p, q]

    @pl.loop(0, n_k)
    def _(k):
        for s in order:
            a_copy(k, s).wait_send()
        x_copy(k).wait_send()
        s_copy(k).wait_send()
        f_copy(k).wait_send()

    for p in range(pieces):
        key_copy(p, r, across, 0).wait_send()
        key_copy(p, r, sib, 1).wait_send()
        key_copy(p, across, sib, 2).wait_send()


def body(tokens, routes, counts, w_gate, w_up):
    n_e = lax.axis_size("expert")
    n_r = lax.axis_size("replica")
    n_tok, width = tokens.shape
    hidden = w_gate.shape[2]
    cap = n_tok * TOP // N_ROUTED
    n_k = 7
    kc = width // n_k
    pieces = 4
    total = n_e * n_r * cap
    sizes = (n_e, n_r, cap, n_tok, n_k, kc, pieces)
    bf = jnp.bfloat16
    dma = pltpu.SemaphoreType.DMA
    vmem = pl.BlockSpec(memory_space=pltpu.VMEM)
    hbm = pl.BlockSpec(memory_space=pl.ANY)
    keys, own = pl.pallas_call(
        functools.partial(exchange_kernel, sizes),
        out_shape=(
            jax.ShapeDtypeStruct((total, n_r * hidden), bf),
            jax.ShapeDtypeStruct((total, hidden), bf),
        ),
        in_specs=[pl.BlockSpec(memory_space=pltpu.SMEM), vmem, hbm, hbm, hbm],
        out_specs=(vmem, vmem),
        scratch_shapes=[
            pltpu.VMEM((n_k, n_tok, kc), bf),
            pltpu.VMEM((n_k, kc, hidden), bf),
            pltpu.VMEM((n_k, kc, hidden), bf),
            pltpu.VMEM((n_k, n_e, cap, kc), bf),
            pltpu.VMEM((n_k, n_r, n_e, cap, kc), bf),
            pltpu.VMEM((total, hidden), jnp.float32),
            pltpu.VMEM((total, hidden), jnp.float32),
            pltpu.VMEM((pieces, n_r, total // pieces, hidden), bf),
            dma((n_k,)), dma((n_k,)), dma((n_k,)),
            dma((n_k, n_e)), dma((n_k, n_e)),
            dma((n_k,)), dma((n_k,)), dma((n_k,)), dma((n_k,)), dma((n_k,)), dma((n_k,)),
            dma((3, pieces)), dma((3, pieces)),
        ],
        compiler_params=pltpu.CompilerParams(
            collective_id=0, has_side_effects=True, vmem_limit_bytes=60 * 1024 * 1024),
        cost_estimate=pl.CostEstimate(
            flops=4 * total * width * hidden,
            bytes_accessed=4 * width * hidden + 2 * n_tok * width,
            transcendentals=total * hidden),
    )(counts, routes.T, tokens, w_gate, w_up)
    factor = 1.0 / (n_e * cap)
    gram = jnp.einsum("rf,rg->fg", own, keys, preferred_element_type=jnp.float32) * factor
    return gram[None]


def solution(mesh):
    return jax.shard_map(
        body,
        mesh=mesh,
        in_specs=(
            P(("expert", "replica"), None),
            P(("expert", "replica"), None),
            P(("expert", "replica")),
            P("expert", None, "replica"),
            P("expert", None, "replica"),
        ),
        out_specs=P("expert", "replica", None),
        check_vma=False,
    )
```

time: 142 us -> 54.6 us (0.38)
  blocking collectives: 90.1 us -> 0 us
  Pallas kernels: 0 us -> 49.6 us
  waiting for transfers between devices: 15.5 us -> 0 us
  between operations: 14.2 us -> 0.66 us
  matrix products: 12.1 us -> 4.06 us
  local copies, waits for them, and re-layouts: 6.31 us -> 0 us
  other arithmetic: 3.17 us -> 0 us
    all_to_all x1 -> x0, blocking collectives: 90.1 us -> none  [body(): lax.all_to_all(replicas, ('expert', 'replica'), split_axis=0, concat_axis...]
    pallas_call x0 -> x1, Pallas kernels: none -> 49.6 us  [body(): pl.pallas_call(functools.partial(exchange_kernel, sizes), out_shape=(jax....]
    all_gather x1 -> x0, waiting for transfers between devices: 15.4 us -> none  [body(): lax.all_gather(own_keys, 'replica', axis=1, tiled=True)]
    dot_general x3 -> x1, matrix products: 12.1 us -> 4.06 us  [body(): jnp.einsum('rf,rg->fg', own, keys, preferred_element_type=jnp.float32)]
    gather x1 -> x0, local copies, waits for them, and re-layouts: 4.47 us -> none  [body(): tokens[source]]
    another operation x2 -> x0, other arithmetic: 2.45 us -> none
  transfers between devices with their start and end apart: 1 -> 0, of which waited for: 1 -> 0; matrix products, arithmetic and copies ran while one was open for 0% -> 0% of each run, Pallas kernels for 0% -> 0%
where the time goes in v1:
time: 54.6 us; the launch traced here: 54.3 us
  Pallas kernels  49.6 us (91%)
  matrix products  4.06 us (7%)
  between operations  0.66 us (1%)
    pallas_call x1, Pallas kernels, body(): pl.pallas_call(functools.partial(exchange_kernel, sizes), out_shape=(jax....  49.6 us
    dot_general x1, matrix products, body(): jnp.einsum('rf,rg->fg', own, keys, preferred_element_type=jnp.float32)  4.06 us

profile of v1, /device:TPU:0, one launch (start us, length us, event | category | flops | bytes accessed | tf_op | source)
XLA Modules:
  0.0 54.3 jit_solution(9148434861231827797)
XLA Ops:
  0.7 49.6 %shard_map.55 = (bf16[256,2048]{1,0:T(8,128)(2,1)}, bf16[256,512]{1,0:T(8,128)(2,1)}) custom-call(s32[1]{0:T(128)S(6)} %copy.6.counts_ref, s32[8,256]{1,0:T(8,128)} %bitcast.5, bf16[256,7168]{1,0:T(8,128)(2,1)} %tokens_hbm.1, bf16[1,7168,512]{2,1,0:T(8,128)(2,1)} %gate_hbm.1, bf16[1,7168,512]{2,1,0:T(8,128)(2,1)} %up_hbm.1), custom_call_target="tpu_custom_call" | custom-call | flops 3758096384 | bytes 18350080 | tf_op jit(solution)/shard_map/pallas_call | solution.py:188
  50.3 4.1 %multiply_bitcast_fusion = f32[1,512,2048]{2,1,0:T(8,128)} fusion(bf16[256,512]{1,0:T(8,128)(2,1)} %get-tuple-element.7, bf16[256,2048]{1,0:T(8,128)(2,1)} %get-tuple-element.8), kind=kOutput, calls=%fused_computation | convolution fusion | flops 537919488 | bytes 5505024 | tf_op jit(solution)/shard_map/rf,rg->fg/dot_general | solution.py:218

commit v2 on v1

--- a/solution.py
+++ b/solution.py
@@ -93,36 +93,41 @@
     half = n_e // 2
     order = sorted(range(1, n_e), key=lambda s: abs(s - half))
 
-    @pl.loop(0, n_k)
-    def _(k):
-        tok_copy(k).wait()
-        picked = jnp.dot(choice, tok[k], preferred_element_type=jnp.float32)
-        slots[k] = picked.reshape(n_e, cap, kc).astype(jnp.bfloat16)
-        for s in order:
-            a_copy(k, s).start()
-        rows[k, r, e] = slots[k, e]
-
     groups = max(1, total_rows // 256)
     per = n_r // groups
     step_rows = total_rows // groups
-
-    @pl.loop(0, n_k + 2)
+    ahead, lag_x, lag_f = 3, 2, 1
+    at_x = ahead + lag_x
+    at_f = at_x + lag_f
+
+    @pl.loop(0, n_k + at_f)
     def _(i):
         @pl.when(i < n_k)
         def _():
+            tok_copy(i).wait()
+            picked = jnp.dot(choice, tok[i], preferred_element_type=jnp.float32)
+            slots[i] = picked.reshape(n_e, cap, kc).astype(jnp.bfloat16)
             for s in order:
-                a_copy(i, s).wait_recv()
-            x_copy(i).start()
-            s_copy(i).start()
-
-        @pl.when((i >= 1) & (i <= n_k))
-        def _():
-            x_copy(i - 1).wait_recv()
-            f_copy(i - 1).start()
-
-        @pl.when(i >= 2)
-        def _():
-            k = i - 2
+                a_copy(i, s).start()
+            rows[i, r, e] = slots[i, e]
+
+        @pl.when((i >= ahead) & (i < n_k + ahead))
+        def _():
+            k = i - ahead
+            for s in order:
+                a_copy(k, s).wait_recv()
+            x_copy(k).start()
+            s_copy(k).start()
+
+        @pl.when((i >= at_x) & (i < n_k + at_x))
+        def _():
+            k = i - at_x
+            x_copy(k).wait_recv()
+            f_copy(k).start()
+
+        @pl.when(i >= at_f)
+        def _():
+            k = i - at_f
             w_copy(gate_hbm, wg, wg_sem, k).wait()
             w_copy(up_hbm, wu, wu_sem, k).wait()
             s_copy(k).wait_recv()
@@ -144,9 +149,9 @@
         u = acc_u[p * piece:(p + 1) * piece, :]
         key = ((g / (1.0 + jnp.exp(-g))) * u).astype(jnp.bfloat16)
         kbuf[p, r] = key
-        own_ref[p * piece:(p + 1) * piece, :] = key
         key_copy(p, r, across, 0).start()
         key_copy(p, r, sib, 1).start()
+    own_ref[...] = kbuf[:, r].reshape(total_rows, hidden).T
     for p in range(pieces):
         key_copy(p, r, across, 0).wait_recv()
         key_copy(p, across, sib, 2).start()
@@ -176,7 +181,7 @@
     n_tok, width = tokens.shape
     hidden = w_gate.shape[2]
     cap = n_tok * TOP // N_ROUTED
-    n_k = 7
+    n_k = 14
     kc = width // n_k
     pieces = 4
     total = n_e * n_r * cap
@@ -189,7 +194,7 @@
         functools.partial(exchange_kernel, sizes),
         out_shape=(
             jax.ShapeDtypeStruct((total, n_r * hidden), bf),
-            jax.ShapeDtypeStruct((total, hidden), bf),
+            jax.ShapeDtypeStruct((hidden, total), bf),
         ),
         in_specs=[pl.BlockSpec(memory_space=pltpu.SMEM), vmem, hbm, hbm, hbm],
         out_specs=(vmem, vmem),
@@ -215,7 +220,7 @@
             transcendentals=total * hidden),
     )(counts, routes.T, tokens, w_gate, w_up)
     factor = 1.0 / (n_e * cap)
-    gram = jnp.einsum("rf,rg->fg", own, keys, preferred_element_type=jnp.float32) * factor
+    gram = jnp.einsum("fr,rg->fg", own, keys, preferred_element_type=jnp.float32) * factor
     return gram[None]
 
 

time: 54.6 us -> 54.4 us (level)
  no operation moved by 1% of the time
where the time goes in v2:
time: 54.4 us; the launch traced here: 54.2 us
  Pallas kernels  49.5 us (91%)
  matrix products  4.04 us (7%)
  between operations  0.66 us (1%)
    pallas_call x1, Pallas kernels, body(): pl.pallas_call(functools.partial(exchange_kernel, sizes), out_shape=(jax....  49.5 us
    dot_general x1, matrix products, body(): jnp.einsum('fr,rg->fg', own, keys, preferred_element_type=jnp.float32)  4.04 us

profile of v2, /device:TPU:0, one launch (start us, length us, event | category | flops | bytes accessed | tf_op | source)
XLA Modules:
  0.0 54.2 jit_solution(4077385096534578057)
XLA Ops:
  0.7 49.5 %shard_map.55 = (bf16[256,2048]{1,0:T(8,128)(2,1)}, bf16[512,256]{1,0:T(8,128)(2,1)}) custom-call(s32[1]{0:T(128)S(6)} %copy.6.counts_ref, s32[8,256]{1,0:T(8,128)} %bitcast.5, bf16[256,7168]{1,0:T(8,128)(2,1)} %tokens_hbm.1, bf16[1,7168,512]{2,1,0:T(8,128)(2,1)} %gate_hbm.1, bf16[1,7168,512]{2,1,0:T(8,128)(2,1)} %up_hbm.1), custom_call_target="tpu_custom_call" | custom-call | flops 3758096384 | bytes 18350080 | tf_op jit(solution)/shard_map/pallas_call | solution.py:193
  50.1 4.0 %multiply_bitcast_fusion = f32[1,512,2048]{2,1,0:T(8,128)} fusion(bf16[512,256]{1,0:T(8,128)(2,1)} %get-tuple-element.7, bf16[256,2048]{1,0:T(8,128)(2,1)} %get-tuple-element.8), kind=kOutput, calls=%fused_computation | convolution fusion | flops 537919488 | bytes 5505024 | tf_op jit(solution)/shard_map/fr,rg->fg/dot_general | solution.py:223

commit v3 on v1

--- a/solution.py
+++ b/solution.py
@@ -21,6 +21,9 @@
     n_e, n_r, cap, n_tok, n_k, kc, pieces = sizes
     total_rows = n_e * n_r * cap
     piece = total_rows // pieces
+    half_rows = total_rows // 2
+    half = n_e // 2
+    n_j = 2 * n_k
     hidden = acc_g.shape[1]
     e = lax.axis_index("expert")
     r = lax.axis_index("replica")
@@ -69,11 +72,12 @@
 
     pl.semaphore_wait(barrier, n_e + 1)
 
-    def a_copy(k, s):
+    def a_copy(j, pos):
+        to = (e + 2 * pos + j // n_k) % n_e
         return pltpu.make_async_remote_copy(
-            src_ref=slots.at[k, (e + s) % n_e], dst_ref=rows.at[k, r, e],
-            send_sem=a_send.at[k, s], recv_sem=a_recv.at[k, s],
-            device_id=((e + s) % n_e, r), device_id_type=MESH)
+            src_ref=slots.at[j % n_k, to], dst_ref=rows.at[j, r, pos],
+            send_sem=a_send.at[j, pos], recv_sem=a_recv.at[j, pos],
+            device_id=(to, r), device_id_type=MESH)
 
     def row_copy(k, who, to, send, recv):
         return pltpu.make_async_remote_copy(
@@ -90,48 +94,8 @@
     def f_copy(k):
         return row_copy(k, across, sib, f_send, f_recv)
 
-    half = n_e // 2
-    order = sorted(range(1, n_e), key=lambda s: abs(s - half))
-
-    @pl.loop(0, n_k)
-    def _(k):
-        tok_copy(k).wait()
-        picked = jnp.dot(choice, tok[k], preferred_element_type=jnp.float32)
-        slots[k] = picked.reshape(n_e, cap, kc).astype(jnp.bfloat16)
-        for s in order:
-            a_copy(k, s).start()
-        rows[k, r, e] = slots[k, e]
-
-    groups = max(1, total_rows // 256)
-    per = n_r // groups
-    step_rows = total_rows // groups
-
-    @pl.loop(0, n_k + 2)
-    def _(i):
-        @pl.when(i < n_k)
-        def _():
-            for s in order:
-                a_copy(i, s).wait_recv()
-            x_copy(i).start()
-            s_copy(i).start()
-
-        @pl.when((i >= 1) & (i <= n_k))
-        def _():
-            x_copy(i - 1).wait_recv()
-            f_copy(i - 1).start()
-
-        @pl.when(i >= 2)
-        def _():
-            k = i - 2
-            w_copy(gate_hbm, wg, wg_sem, k).wait()
-            w_copy(up_hbm, wu, wu_sem, k).wait()
-            s_copy(k).wait_recv()
-            f_copy(k).wait_recv()
-            for g in range(groups):
-                block = rows[k, g * per:(g + 1) * per].reshape(step_rows, kc)
-                at = slice(g * step_rows, (g + 1) * step_rows)
-                acc_g[at, :] += jnp.dot(block, wg[k], preferred_element_type=jnp.float32)
-                acc_u[at, :] += jnp.dot(block, wu[k], preferred_element_type=jnp.float32)
+    order = sorted(range(half), key=lambda pos: abs(2 * pos - half))
+    remote = [pos for pos in order if pos > 0]
 
     def key_copy(p, who, to, n):
         return pltpu.make_async_remote_copy(
@@ -139,35 +103,127 @@
             send_sem=k_send.at[n, p], recv_sem=k_recv.at[n, p],
             device_id=(e, to), device_id_type=MESH)
 
-    for p in range(pieces):
-        g = acc_g[p * piece:(p + 1) * piece, :]
-        u = acc_u[p * piece:(p + 1) * piece, :]
-        key = ((g / (1.0 + jnp.exp(-g))) * u).astype(jnp.bfloat16)
-        kbuf[p, r] = key
-        own_ref[p * piece:(p + 1) * piece, :] = key
-        key_copy(p, r, across, 0).start()
-        key_copy(p, r, sib, 1).start()
-    for p in range(pieces):
-        key_copy(p, r, across, 0).wait_recv()
-        key_copy(p, across, sib, 2).start()
-    for p in range(pieces):
-        key_copy(p, r, sib, 1).wait_recv()
-        key_copy(p, across, sib, 2).wait_recv()
-        for q in range(n_r):
-            keys_ref[p * piece:(p + 1) * piece, q * hidden:(q + 1) * hidden] = kbuf[p, q]
-
-    @pl.loop(0, n_k)
-    def _(k):
-        for s in order:
-            a_copy(k, s).wait_send()
-        x_copy(k).wait_send()
-        s_copy(k).wait_send()
-        f_copy(k).wait_send()
+    def finish_keys(h):
+        for q in range(pieces // 2):
+            p = h * (pieces // 2) + q
+            g = acc_g[q * piece:(q + 1) * piece, :]
+            u = acc_u[q * piece:(q + 1) * piece, :]
+            kbuf[p, r] = ((g / (1.0 + jnp.exp(-g))) * u).astype(jnp.bfloat16)
+            key_copy(p, r, across, 0).start()
+            key_copy(p, r, sib, 1).start()
+
+    def relay_keys(h):
+        for q in range(pieces // 2):
+            p = h * (pieces // 2) + q
+            key_copy(p, r, across, 0).wait_recv()
+            key_copy(p, across, sib, 2).start()
+
+    def place_keys(h):
+        for q in range(pieces // 2):
+            p = h * (pieces // 2) + q
+            key_copy(p, r, sib, 1).wait_recv()
+            key_copy(p, across, sib, 2).wait_recv()
+            for o in range(n_r):
+                keys_ref[p * piece:(p + 1) * piece, o * hidden:(o + 1) * hidden] = kbuf[p, o]
+
+    groups = max(1, half_rows // 256)
+    per = n_r // groups
+    step_rows = half_rows // groups
+    ahead, lag_x, lag_f = 3, 2, 1
+    at_x = ahead + lag_x
+    at_f = at_x + lag_f
+
+    @pl.loop(0, n_j + at_f)
+    def _(i):
+        @pl.when(i < n_k)
+        def _():
+            tok_copy(i).wait()
+            picked = jnp.dot(choice, tok[i], preferred_element_type=jnp.float32)
+            slots[i] = picked.reshape(n_e, cap, kc).astype(jnp.bfloat16)
+            for pos in remote:
+                a_copy(i, pos).start()
+            rows[i, r, 0] = slots[i, e]
+
+        @pl.when((i >= n_k) & (i < n_j))
+        def _():
+            for pos in order:
+                a_copy(i, pos).start()
+
+        @pl.when((i >= ahead) & (i < n_j + ahead))
+        def _():
+            j = i - ahead
+            for pos in remote:
+                a_copy(j, pos).wait_recv()
+
+            @pl.when(j >= n_k)
+            def _():
+                a_copy(j, 0).wait_recv()
+
+            x_copy(j).start()
+            s_copy(j).start()
+
+        @pl.when((i >= at_x) & (i < n_j + at_x))
+        def _():
+            j = i - at_x
+            x_copy(j).wait_recv()
+            f_copy(j).start()
+
+        @pl.when(i >= at_f)
+        def _():
+            j = i - at_f
+            k = j % n_k
+
+            @pl.when(j < n_k)
+            def _():
+                w_copy(gate_hbm, wg, wg_sem, k).wait()
+                w_copy(up_hbm, wu, wu_sem, k).wait()
+
+            s_copy(j).wait_recv()
+            f_copy(j).wait_recv()
+            for g in range(groups):
+                block = rows[j, g * per:(g + 1) * per].reshape(step_rows, kc)
+                at = slice(g * step_rows, (g + 1) * step_rows)
+                acc_g[at, :] += jnp.dot(block, wg[k], preferred_element_type=jnp.float32)
+                acc_u[at, :] += jnp.dot(block, wu[k], preferred_element_type=jnp.float32)
+
+        @pl.when(i == at_f + n_k - 1)
+        def _():
+            finish_keys(0)
+            acc_g[...] = jnp.zeros_like(acc_g)
+            acc_u[...] = jnp.zeros_like(acc_u)
+
+        @pl.when(i == at_f + n_k + 3)
+        def _():
+            relay_keys(0)
+
+    finish_keys(1)
+    place_keys(0)
+    own_ref[...] = kbuf[:, r].reshape(total_rows, hidden).T
+    relay_keys(1)
+    place_keys(1)
+
+    @pl.loop(0, n_j)
+    def _(j):
+        for pos in remote:
+            a_copy(j, pos).wait_send()
+
+        @pl.when(j >= n_k)
+        def _():
+            a_copy(j, 0).wait_send()
+
+        x_copy(j).wait_send()
+        s_copy(j).wait_send()
+        f_copy(j).wait_send()
 
     for p in range(pieces):
         key_copy(p, r, across, 0).wait_send()
         key_copy(p, r, sib, 1).wait_send()
         key_copy(p, across, sib, 2).wait_send()
+
+
+def gram_kernel(factor, own_ref, keys_ref, out_ref):
+    out_ref[...] = jnp.dot(
+        own_ref[...], keys_ref[...], preferred_element_type=jnp.float32) * factor
 
 
 def body(tokens, routes, counts, w_gate, w_up):
@@ -189,7 +245,7 @@
         functools.partial(exchange_kernel, sizes),
         out_shape=(
             jax.ShapeDtypeStruct((total, n_r * hidden), bf),
-            jax.ShapeDtypeStruct((total, hidden), bf),
+            jax.ShapeDtypeStruct((hidden, total), bf),
         ),
         in_specs=[pl.BlockSpec(memory_space=pltpu.SMEM), vmem, hbm, hbm, hbm],
         out_specs=(vmem, vmem),
@@ -198,13 +254,14 @@
             pltpu.VMEM((n_k, kc, hidden), bf),
             pltpu.VMEM((n_k, kc, hidden), bf),
             pltpu.VMEM((n_k, n_e, cap, kc), bf),
-            pltpu.VMEM((n_k, n_r, n_e, cap, kc), bf),
-            pltpu.VMEM((total, hidden), jnp.float32),
-            pltpu.VMEM((total, hidden), jnp.float32),
+            pltpu.VMEM((2 * n_k, n_r, n_e // 2, cap, kc), bf),
+            pltpu.VMEM((total // 2, hidden), jnp.float32),
+            pltpu.VMEM((total // 2, hidden), jnp.float32),
             pltpu.VMEM((pieces, n_r, total // pieces, hidden), bf),
             dma((n_k,)), dma((n_k,)), dma((n_k,)),
-            dma((n_k, n_e)), dma((n_k, n_e)),
-            dma((n_k,)), dma((n_k,)), dma((n_k,)), dma((n_k,)), dma((n_k,)), dma((n_k,)),
+            dma((2 * n_k, n_e // 2)), dma((2 * n_k, n_e // 2)),
+            dma((2 * n_k,)), dma((2 * n_k,)), dma((2 * n_k,)),
+            dma((2 * n_k,)), dma((2 * n_k,)), dma((2 * n_k,)),
             dma((3, pieces)), dma((3, pieces)),
         ],
         compiler_params=pltpu.CompilerParams(
@@ -215,7 +272,21 @@
             transcendentals=total * hidden),
     )(counts, routes.T, tokens, w_gate, w_up)
     factor = 1.0 / (n_e * cap)
-    gram = jnp.einsum("rf,rg->fg", own, keys, preferred_element_type=jnp.float32) * factor
+    gram = pl.pallas_call(
+        functools.partial(gram_kernel, factor),
+        grid=(n_r,),
+        out_shape=jax.ShapeDtypeStruct((hidden, n_r * hidden), jnp.float32),
+        in_specs=[
+            pl.BlockSpec((hidden, total), lambda c: (0, 0)),
+            pl.BlockSpec((total, hidden), lambda c: (0, c)),
+        ],
+        out_specs=pl.BlockSpec((hidden, hidden), lambda c: (0, c)),
+        compiler_params=pltpu.CompilerParams(vmem_limit_bytes=32 * 1024 * 1024),
+        cost_estimate=pl.CostEstimate(
+            flops=2 * total * hidden * hidden * n_r,
+            bytes_accessed=4 * n_r * hidden * hidden + 2 * total * hidden * (n_r + 1),
+            transcendentals=0),
+    )(own, keys)
     return gram[None]
 
 

time: 54.6 us -> 53.2 us (0.974)
  matrix products: 4.06 us -> 0 us
  local copies, waits for them, and re-layouts: 0 us -> 2.17 us
    dot_general x1 -> x0, matrix products: 4.06 us -> none  [body(): jnp.einsum('rf,rg->fg', own, keys, preferred_element_type=jnp.float32)]
    pallas_call x0 -> x1, Pallas kernels: none -> 2.95 us  [body(): pl.pallas_call(functools.partial(gram_kernel, factor), grid=(n_r,), out_s...]
    pallas_call x1, Pallas kernels: 49.6 us -> 47.2 us  [body(): pl.pallas_call(functools.partial(exchange_kernel, sizes), out_shape=(jax....]
    unnamed x0 -> x4, local copies, waits for them, and re-layouts: none -> 2.17 us
where the time goes in v3:
time: 53.2 us; the launch traced here: 52.9 us
  Pallas kernels  50.1 us (94%)
  local copies, waits for them, and re-layouts  2.17 us (4%)
  between operations  0.67 us (1%)
    pallas_call x1, Pallas kernels, body(): pl.pallas_call(functools.partial(exchange_kernel, sizes), out_shape=(jax....  47.2 us
    pallas_call x1, Pallas kernels, body(): pl.pallas_call(functools.partial(gram_kernel, factor), grid=(n_r,), out_s...  2.95 us
    unnamed x4, local copies, waits for them, and re-layouts  2.17 us

profile of v3, /device:TPU:0, one launch (start us, length us, event | category | flops | bytes accessed | tf_op | source)
XLA Modules:
  0.0 52.9 jit_solution(3221669393518166924)
XLA Ops:
  0.7 47.2 %shard_map.55 = (bf16[256,2048]{1,0:T(8,128)(2,1)}, bf16[512,256]{1,0:T(8,128)(2,1)}) custom-call(s32[1]{0:T(128)S(6)} %copy.6.counts_ref, s32[8,256]{1,0:T(8,128)} %bitcast.2, bf16[256,7168]{1,0:T(8,128)(2,1)} %tokens_hbm.1, bf16[1,7168,512]{2,1,0:T(8,128)(2,1)} %gate_hbm.1, bf16[1,7168,512]{2,1,0:T(8,128)(2,1)} %up_hbm.1), custom_call_target="tpu_custom_call" | custom-call | flops 3758096384 | bytes 18350080 | tf_op jit(solution)/shard_map/pallas_call | solution.py:244
  47.8 0.0 copy-start
  47.8 1.2 %copy-done = bf16[256,2048]{1,0:T(8,128)(2,1)S(1)} copy-done((bf16[256,2048]{1,0:T(8,128)(2,1)S(1)}, bf16[256,2048]{1,0:T(8,128)(2,1)}, u32[]{:S(2)}) %copy-start) | copy-done | bytes 1048600
  49.0 0.0 copy-start.1
  49.0 0.9 %copy-done.1 = bf16[512,256]{1,0:T(8,128)(2,1)S(1)} copy-done((bf16[512,256]{1,0:T(8,128)(2,1)S(1)}, bf16[512,256]{1,0:T(8,128)(2,1)}, u32[]{:S(2)}) %copy-start.1) | copy-done | bytes 262168
  50.0 2.9 %shard_map.56 = f32[512,2048]{1,0:T(8,128)} custom-call(bf16[512,256]{1,0:T(8,128)(2,1)S(1)} %copy-done.1, bf16[256,2048]{1,0:T(8,128)(2,1)S(1)} %copy-done), custom_call_target="tpu_custom_call" | custom-call | flops 536870912 | bytes 5505024 | tf_op jit(solution)/shard_map/pallas_call | solution.py:275
Async XLA Ops:
  47.8 1.2 %copy-start = (bf16[256,2048]{1,0:T(8,128)(2,1)S(1)}, bf16[256,2048]{1,0:T(8,128)(2,1)}, u32[]{:S(2)}) copy-start(bf16[256,2048]{1,0:T(8,128)(2,1)} %get-tuple-element.8.keys_ref) | copy-start | bytes 3145732
  49.0 0.9 %copy-start.1 = (bf16[512,256]{1,0:T(8,128)(2,1)S(1)}, bf16[512,256]{1,0:T(8,128)(2,1)}, u32[]{:S(2)}) copy-start(bf16[512,256]{1,0:T(8,128)(2,1)} %get-tuple-element.7.own_ref) | copy-start | bytes 786436

commit v4 on v3

--- a/solution.py
+++ b/solution.py
@@ -16,7 +16,7 @@
     sizes, counts_ref, routes_ref, tokens_hbm, gate_hbm, up_hbm, keys_ref, own_ref,
     tok, wg, wu, slots, rows, acc_g, acc_u, kbuf,
     tok_sem, wg_sem, wu_sem, a_send, a_recv, x_send, x_recv, s_send, s_recv,
-    f_send, f_recv, k_send, k_recv,
+    f_send, f_recv, k_send, k_recv, l_send, l_recv,
 ):
     n_e, n_r, cap, n_tok, n_k, kc, pieces = sizes
     total_rows = n_e * n_r * cap
@@ -45,9 +45,6 @@
 
     for k in range(n_k):
         tok_copy(k).start()
-    for k in range(n_k):
-        w_copy(gate_hbm, wg, wg_sem, k).start()
-        w_copy(up_hbm, wu, wu_sem, k).start()
 
     n_s = n_e * cap
     count = counts_ref[0]
@@ -88,6 +85,18 @@
     def x_copy(k):
         return row_copy(k, r, across, x_send, x_recv)
 
+    def l_copy(k):
+        return pltpu.make_async_remote_copy(
+            src_ref=rows.at[k, r, 0], dst_ref=rows.at[k, r, 0],
+            send_sem=l_send.at[k], recv_sem=l_recv.at[k],
+            device_id=(e, across), device_id_type=MESH)
+
+    def y_copy(k):
+        return pltpu.make_async_remote_copy(
+            src_ref=rows.at[k, r, pl.ds(1, half - 1)], dst_ref=rows.at[k, r, pl.ds(1, half - 1)],
+            send_sem=x_send.at[k], recv_sem=x_recv.at[k],
+            device_id=(e, across), device_id_type=MESH)
+
     def s_copy(k):
         return row_copy(k, r, sib, s_send, s_recv)
 
@@ -143,6 +152,9 @@
             for pos in remote:
                 a_copy(i, pos).start()
             rows[i, r, 0] = slots[i, e]
+            l_copy(i).start()
+            w_copy(gate_hbm, wg, wg_sem, i).start()
+            w_copy(up_hbm, wu, wu_sem, i).start()
 
         @pl.when((i >= n_k) & (i < n_j))
         def _():
@@ -158,14 +170,27 @@
             @pl.when(j >= n_k)
             def _():
                 a_copy(j, 0).wait_recv()
-
-            x_copy(j).start()
+                x_copy(j).start()
+
+            @pl.when(j < n_k)
+            def _():
+                y_copy(j).start()
+
             s_copy(j).start()
 
         @pl.when((i >= at_x) & (i < n_j + at_x))
         def _():
             j = i - at_x
-            x_copy(j).wait_recv()
+
+            @pl.when(j < n_k)
+            def _():
+                l_copy(j).wait_recv()
+                y_copy(j).wait_recv()
+
+            @pl.when(j >= n_k)
+            def _():
+                x_copy(j).wait_recv()
+
             f_copy(j).start()
 
         @pl.when(i >= at_f)
@@ -210,8 +235,13 @@
         @pl.when(j >= n_k)
         def _():
             a_copy(j, 0).wait_send()
-
-        x_copy(j).wait_send()
+            x_copy(j).wait_send()
+
+        @pl.when(j < n_k)
+        def _():
+            l_copy(j).wait_send()
+            y_copy(j).wait_send()
+
         s_copy(j).wait_send()
         f_copy(j).wait_send()
 
@@ -262,7 +292,7 @@
             dma((2 * n_k, n_e // 2)), dma((2 * n_k, n_e // 2)),
             dma((2 * n_k,)), dma((2 * n_k,)), dma((2 * n_k,)),
             dma((2 * n_k,)), dma((2 * n_k,)), dma((2 * n_k,)),
-            dma((3, pieces)), dma((3, pieces)),
+            dma((3, pieces)), dma((3, pieces)), dma((n_k,)), dma((n_k,)),
         ],
         compiler_params=pltpu.CompilerParams(
             collective_id=0, has_side_effects=True, vmem_limit_bytes=60 * 1024 * 1024),
@@ -281,7 +311,7 @@
             pl.BlockSpec((total, hidden), lambda c: (0, c)),
         ],
         out_specs=pl.BlockSpec((hidden, hidden), lambda c: (0, c)),
-        compiler_params=pltpu.CompilerParams(vmem_limit_bytes=32 * 1024 * 1024),
+        compiler_params=pltpu.CompilerParams(vmem_limit_bytes=60 * 1024 * 1024),
         cost_estimate=pl.CostEstimate(
             flops=2 * total * hidden * hidden * n_r,
             bytes_accessed=4 * n_r * hidden * hidden + 2 * total * hidden * (n_r + 1),

time: 53.2 us -> 53.1 us (level)
  local copies, waits for them, and re-layouts: 2.17 us -> 0 us
  Pallas kernels: 50.1 us -> 52.2 us
    unnamed x4 -> x0, local copies, waits for them, and re-layouts: 2.17 us -> none
    pallas_call x1, Pallas kernels: 2.95 us -> 4.54 us  [body(): pl.pallas_call(functools.partial(gram_kernel, factor), grid=(n_r,), out_s...]
where the time goes in v4:
time: 53.1 us; the launch traced here: 52.8 us
  Pallas kernels  52.2 us (98%)
  between operations  0.66 us (1%)
    pallas_call x1, Pallas kernels, body(): pl.pallas_call(functools.partial(exchange_kernel, sizes), out_shape=(jax....  47.6 us
    pallas_call x1, Pallas kernels, body(): pl.pallas_call(functools.partial(gram_kernel, factor), grid=(n_r,), out_s...  4.54 us

profile of v4, /device:TPU:0, one launch (start us, length us, event | category | flops | bytes accessed | tf_op | source)
XLA Modules:
  0.0 52.8 jit_solution(9425516067335330406)
XLA Ops:
  0.7 47.6 %shard_map.55 = (bf16[256,2048]{1,0:T(8,128)(2,1)}, bf16[512,256]{1,0:T(8,128)(2,1)}) custom-call(s32[1]{0:T(128)S(6)} %copy.6.counts_ref, s32[8,256]{1,0:T(8,128)} %bitcast.2, bf16[256,7168]{1,0:T(8,128)(2,1)} %tokens_hbm.1, bf16[1,7168,512]{2,1,0:T(8,128)(2,1)} %gate_hbm.1, bf16[1,7168,512]{2,1,0:T(8,128)(2,1)} %up_hbm.1), custom_call_target="tpu_custom_call" | custom-call | flops 3758096384 | bytes 18350080 | tf_op jit(solution)/shard_map/pallas_call | solution.py:274
  48.3 4.5 %shard_map.56 = f32[512,2048]{1,0:T(8,128)} custom-call(bf16[512,256]{1,0:T(8,128)(2,1)} %get-tuple-element.7.own_ref, bf16[256,2048]{1,0:T(8,128)(2,1)} %get-tuple-element.8.keys_ref), custom_call_target="tpu_custom_call" | custom-call | flops 536870912 | bytes 5505024 | tf_op jit(solution)/shard_map/pallas_call | solution.py:305

commit v5 on v4

--- a/solution.py
+++ b/solution.py
@@ -304,13 +304,13 @@
     factor = 1.0 / (n_e * cap)
     gram = pl.pallas_call(
         functools.partial(gram_kernel, factor),
-        grid=(n_r,),
+        grid=(2 * n_r,),
         out_shape=jax.ShapeDtypeStruct((hidden, n_r * hidden), jnp.float32),
         in_specs=[
             pl.BlockSpec((hidden, total), lambda c: (0, 0)),
-            pl.BlockSpec((total, hidden), lambda c: (0, c)),
+            pl.BlockSpec((total, hidden // 2), lambda c: (0, c)),
         ],
-        out_specs=pl.BlockSpec((hidden, hidden), lambda c: (0, c)),
+        out_specs=pl.BlockSpec((hidden, hidden // 2), lambda c: (0, c)),
         compiler_params=pltpu.CompilerParams(vmem_limit_bytes=60 * 1024 * 1024),
         cost_estimate=pl.CostEstimate(
             flops=2 * total * hidden * hidden * n_r,

time: 53.1 us -> 55.3 us (1.041)
  Pallas kernels: 52.2 us -> 54.3 us
    pallas_call x1, Pallas kernels: 4.54 us -> 6.7 us  [body(): pl.pallas_call(functools.partial(gram_kernel, factor), grid=(2 * n_r,), o...]
where the time goes in v5:
time: 55.3 us; the launch traced here: 55 us
  Pallas kernels  54.3 us (98%)
  between operations  0.66 us (1%)
    pallas_call x1, Pallas kernels, body(): pl.pallas_call(functools.partial(exchange_kernel, sizes), out_shape=(jax....  47.6 us
    pallas_call x1, Pallas kernels, body(): pl.pallas_call(functools.partial(gram_kernel, factor), grid=(2 * n_r,), o...  6.7 us

profile of v5, /device:TPU:0, one launch (start us, length us, event | category | flops | bytes accessed | tf_op | source)
XLA Modules:
  0.0 55.0 jit_solution(5961527582435709658)
XLA Ops:
  0.7 47.6 %shard_map.55 = (bf16[256,2048]{1,0:T(8,128)(2,1)}, bf16[512,256]{1,0:T(8,128)(2,1)}) custom-call(s32[1]{0:T(128)S(6)} %copy.6.counts_ref, s32[8,256]{1,0:T(8,128)} %bitcast.2, bf16[256,7168]{1,0:T(8,128)(2,1)} %tokens_hbm.1, bf16[1,7168,512]{2,1,0:T(8,128)(2,1)} %gate_hbm.1, bf16[1,7168,512]{2,1,0:T(8,128)(2,1)} %up_hbm.1), custom_call_target="tpu_custom_call" | custom-call | flops 3758096384 | bytes 18350080 | tf_op jit(solution)/shard_map/pallas_call | solution.py:274
  48.3 6.7 %shard_map.56 = f32[512,2048]{1,0:T(8,128)} custom-call(bf16[512,256]{1,0:T(8,128)(2,1)} %get-tuple-element.7.own_ref, bf16[256,2048]{1,0:T(8,128)(2,1)} %get-tuple-element.8.keys_ref), custom_call_target="tpu_custom_call" | custom-call | flops 536870912 | bytes 5505024 | tf_op jit(solution)/shard_map/pallas_call | solution.py:305
